TPU v7x, 32 devices: a whole 2x2x4 slice. The times are simulated.
32 devices in a mesh: groups: 2 (over y), dp: 4 (over z), fsdp: 2 (over x), adapter: 2 (over core).
Axes of the slice: x: 2, y: 2, z: 4, core: 2. Of those that a mesh axis runs over, the one named last changes fastest.
Arguments:
- output_gradient: bfloat16 [3072, 8192], P(('groups', 'dp'), ('fsdp', 'adapter')), parts along dimension 0, may hold values from -4 to 4
- attention_output: bfloat16 [3072, 4096], P(('groups', 'dp'), ('fsdp', 'adapter')), parts along dimension 0, may hold values from -6 to 6
- frozen_weight: bfloat16 [4096, 8192], P(('fsdp', 'adapter'), 'dp'), may hold values from -0.0625 to 0.0625
- adapter_down_table: bfloat16 [256, 4096, 16], P(('groups', 'dp'), ('fsdp', 'adapter')), parts along dimension 0, may hold values from -1.5 to 1.5
- adapter_up_table: bfloat16 [256, 16, 8192], P(('groups', 'dp'), None, ('fsdp', 'adapter')), parts along dimension 0, may hold values from -0.0625 to 0.0625
- segment_adapter: int32 [16], P(('groups', 'dp')), parts along dimension 0, may hold values from 0 to 127, as said below
- segment_first_token: int32 [16], P(('groups', 'dp')), parts along dimension 0, may hold values from 0 to 383, as said below
- adapter_table_row: int32 [256], P('groups'), parts along dimension 0, may hold values from 0 to 127, as said below
Outputs:
- input_gradient: bfloat16 [3072, 4096], P(('groups', 'dp'), ('fsdp', 'adapter')), parts along dimension 0
- grad_a: bfloat16 [256, 4096, 16], P(('groups', 'dp'), ('fsdp', 'adapter')), parts along dimension 0
- grad_b: bfloat16 [256, 16, 8192], P(('groups', 'dp'), None, ('fsdp', 'adapter')), parts along dimension 0
There are 2 independent parts, one for each index of `groups`. A program takes and returns all parts, laid end to end along the dimension named above; an argument that names none is the same for every part. Nothing has to cross between parts.
Inputs may be any that keep to these rules, and one draw needn't show every extreme that they name: `segment_adapter`: the 2 segments of one dp index name adapters whose table rows lie in the blocks of 32 rows of 2 different dp indices. `segment_first_token`: within each dp index, 2 increasing offsets with the first 0. `adapter_table_row`: a permutation of the table rows.
All inputs are finite; a program needn't handle non-finite values.
Results may differ from a plain program's by a relative error of at most 0.0049.
Values may be sent and summed in bfloat16 or wider, within the bound.
A program may use at most 128 MiB of HBM per device.

v0:
```python
import jax
import jax.numpy as jnp
from jax import lax
from jax.sharding import PartitionSpec as P

adapter_scale = 2.0


def local(
    output_gradient,
    attention_output,
    frozen_weight,
    adapter_down_table,
    adapter_up_table,
    segment_adapter,
    segment_first_token,
    adapter_table_row,
):
    n_dp = lax.axis_size("dp")
    segs = segment_adapter.shape[0]
    tok_rows = output_gradient.shape[0]
    adapters_per_device, features_local, rank_width = adapter_down_table.shape
    width_local = adapter_up_table.shape[2]
    brain_float_half = jnp.bfloat16
    hits = (
        segment_adapter[:, None] == jnp.arange(adapter_table_row.shape[0], dtype=jnp.int32)[None, :]
    )
    table_rows = jnp.sum(jnp.where(hits, adapter_table_row[None, :], 0), axis=1)
    owners = table_rows // adapters_per_device
    local_rows = table_rows % adapters_per_device
    to_owner = owners[:, None] == jnp.arange(n_dp, dtype=jnp.int32)[None, :]
    asked = jnp.sum(jnp.where(to_owner, (local_rows + 1)[:, None], 0), axis=0)
    wanted = lax.all_to_all(asked, "dp", split_axis=0, concat_axis=0, tiled=True)
    segment_selector = (
        wanted[:, None] - 1 == jnp.arange(adapters_per_device, dtype=jnp.int32)[None, :]
    ).astype(brain_float_half)
    send_a = jnp.dot(
        segment_selector,
        adapter_down_table.reshape(adapters_per_device, features_local * rank_width),
        preferred_element_type=jnp.float32,
    ).astype(brain_float_half)
    send_b = jnp.dot(
        segment_selector,
        adapter_up_table.reshape(adapters_per_device, rank_width * width_local),
        preferred_element_type=jnp.float32,
    ).astype(brain_float_half)
    got_a, got_b = (
        lax.all_to_all(send_a, "dp", split_axis=0, concat_axis=0, tiled=True),
        lax.all_to_all(send_b, "dp", split_axis=0, concat_axis=0, tiled=True),
    )
    chooser = to_owner.astype(brain_float_half)
    seg_factor_a = (
        jnp.dot(chooser, got_a, preferred_element_type=jnp.float32)
        .astype(brain_float_half)
        .reshape(segs, features_local, rank_width)
    )
    stacked_b = (
        jnp.dot(chooser, got_b, preferred_element_type=jnp.float32)
        .astype(brain_float_half)
        .reshape(segs * rank_width, width_local)
    )
    stacked_a = jnp.transpose(seg_factor_a, (1, 0, 2)).reshape(features_local, segs * rank_width)
    places = jnp.arange(tok_rows, dtype=jnp.int32)
    seg_of = (
        jnp.sum((places[:, None] >= segment_first_token[None, :]).astype(jnp.int32), axis=1) - 1
    )
    member = seg_of[:, None] == jnp.arange(segs, dtype=jnp.int32)[None, :]
    member_cols = jnp.repeat(member, rank_width, axis=1)
    up_part = lax.dot_general(
        output_gradient, stacked_b, (((1,), (1,)), ((), ())), preferred_element_type=jnp.float32
    )
    down_part = jnp.dot(attention_output, stacked_a, preferred_element_type=jnp.float32)
    up_proj, down_proj = lax.psum((up_part, down_part), ("fsdp", "adapter"))
    up_factor_block = jnp.where(member_cols, up_proj, 0.0).astype(brain_float_half)
    down_factor_block = jnp.where(member_cols, down_proj, 0.0).astype(brain_float_half)
    whole_grad = lax.all_gather(output_gradient, ("fsdp", "adapter"), axis=1, tiled=True)
    frozen_output = lax.dot_general(
        whole_grad,
        lax.all_gather(frozen_weight, "dp", axis=1, tiled=True),
        (((1,), (1,)), ((), ())),
        preferred_element_type=jnp.float32,
    )
    adapter_extra = lax.dot_general(
        up_factor_block, stacked_a, (((1,), (1,)), ((), ())), preferred_element_type=jnp.float32
    )
    input_gradient = (frozen_output + adapter_scale * adapter_extra).astype(brain_float_half)
    seg_grad_a = (
        adapter_scale
        * lax.dot_general(
            attention_output,
            up_factor_block,
            (((0,), (0,)), ((), ())),
            preferred_element_type=jnp.float32,
        )
    ).astype(brain_float_half)
    seg_grad_a = jnp.transpose(
        seg_grad_a.reshape(features_local, segs, rank_width), (1, 0, 2)
    ).reshape(segs, features_local * rank_width)
    seg_grad_b = (
        adapter_scale
        * lax.dot_general(
            down_factor_block,
            output_gradient,
            (((0,), (0,)), ((), ())),
            preferred_element_type=jnp.float32,
        )
    ).astype(brain_float_half)
    seg_grad_b = seg_grad_b.reshape(segs, rank_width * width_local)
    placer = jnp.transpose(chooser)
    out_a = jnp.dot(placer, seg_grad_a, preferred_element_type=jnp.float32).astype(brain_float_half)
    out_b = jnp.dot(placer, seg_grad_b, preferred_element_type=jnp.float32).astype(brain_float_half)
    back_a, back_b = (
        lax.all_to_all(out_a, "dp", split_axis=0, concat_axis=0, tiled=True),
        lax.all_to_all(out_b, "dp", split_axis=0, concat_axis=0, tiled=True),
    )
    gatherer = jnp.transpose(segment_selector)
    grad_a = (
        jnp.dot(gatherer, back_a, preferred_element_type=jnp.float32)
        .astype(brain_float_half)
        .reshape(adapters_per_device, features_local, rank_width)
    )
    grad_b = (
        jnp.dot(gatherer, back_b, preferred_element_type=jnp.float32)
        .astype(brain_float_half)
        .reshape(adapters_per_device, rank_width, width_local)
    )
    return (input_gradient, grad_a, grad_b)


def solution(mesh):
    in_specs = (
        P(("groups", "dp"), ("fsdp", "adapter")),
        P(("groups", "dp"), ("fsdp", "adapter")),
        P(("fsdp", "adapter"), "dp"),
        P(("groups", "dp"), ("fsdp", "adapter"), None),
        P(("groups", "dp"), None, ("fsdp", "adapter")),
        P(("groups", "dp")),
        P(("groups", "dp")),
        P("groups"),
    )
    out_specs = (
        P(("groups", "dp"), ("fsdp", "adapter")),
        P(("groups", "dp"), ("fsdp", "adapter"), None),
        P(("groups", "dp"), None, ("fsdp", "adapter")),
    )
    return jax.shard_map(local, mesh=mesh, in_specs=in_specs, out_specs=out_specs, check_vma=False)
```

profile of v0, /device:TPU:0, one launch (start us, length us, event | category | flops | bytes accessed | tf_op | source)
XLA Modules:
  0.0 374.4 jit_solution(15754895048860130620)
XLA Ops:
  7.2 0.0 copy-start
  7.2 0.0 all-gather.3.cloned.1.call-start
  7.2 0.7 all-gather.3.cloned.1.call-update
  7.9 0.0 copy-start.3
  7.9 0.0 all-gather.5.cloned.1.call-start
  8.0 0.7 all-gather.5.cloned.1.call-update
  8.7 0.2 fusion.17
  8.9 0.1 select_reduce_fusion
  9.0 0.7 copy.37
  9.7 6.3 %all-to-all-start = ((s32[4,1,1]{2,1,0:T(1,128)}), s32[4,1,1]{2,1,0:T(1,128)S(1)}, u32[]{:S(2)}, u32[]{:S(2)}) async-start(s32[4,1,1]{2,1,0:T(1,128)} %copy.37), calls=%async_computation | async-start | bytes 4096 | tf_op jit(solution)/shard_map/all_to_all | solution.py:33
  16.0 2.7 copy.51
  18.7 0.0 copy-start.2
  18.7 7.4 %copy.39 = bf16[32,1024,16]{0,2,1:T(8,128)(2,1)} copy(bf16[32,1024,16]{1,2,0:T(8,128)(2,1)} %param.11) | data formatting | bytes 2097152 | tf_op args[3]
  26.1 0.0 copy-done.2
  26.1 0.1 fusion.16
  26.3 0.0 all-to-all-done
  26.3 0.2 add_reduce_fusion
  26.4 3.4 fusion.2
  29.8 0.5 broadcast.109
  30.4 0.8 reduce.3
  31.2 0.8 reshape.108
  32.0 5.1 %all-to-all-start.2 = ((bf16[4,2,8192]{2,1,0:T(2,128)(2,1)}), bf16[4,2,8192]{2,1,0:T(2,128)(2,1)S(1)}, u32[]{:S(2)}, u32[]{:S(2)}) async-start(bf16[4,2,8192]{2,1,0:T(2,128)(2,1)} %reshape.108), calls=%async_computation.2 | async-start | bytes 262144 | tf_op jit(solution)/shard_map/all_to_all | solution.py:48
  37.1 0.5 fusion
  37.5 1.0 reduce.2
  38.5 1.0 reshape.106
  39.5 3.5 all-to-all-done.2
  43.0 3.4 all-to-all-start.1
  46.4 0.1 reshape.109
  46.5 0.0 copy-start.1
  46.6 0.3 convolution_convert_fusion.7
  46.9 0.4 reshape.98
  47.3 0.2 copy.41
  47.4 0.3 convolution_bitcast_fusion
  47.8 5.4 %all-to-all-done.1 = bf16[4,2,16384]{2,1,0:T(2,128)(2,1)S(1)} async-done(((bf16[4,2,16384]{2,1,0:T(2,128)(2,1)}), bf16[4,2,16384]{2,1,0:T(2,128)(2,1)S(1)}, u32[]{:S(2)}, u32[]{:S(2)}) %all-to-all-start.1) | async-done | bytes 262176 | tf_op jit(solution)/shard_map/all_to_all | solution.py:49
  53.2 0.3 reshape.107
  53.4 0.4 convolution_convert_fusion.3
  53.9 0.1 reshape.96
  54.0 0.6 convolution_bitcast_fusion.1
  54.5 11.1 %all-reduce = (bf16[384,32]{0,1:T(8,128)(2,1)S(1)}, bf16[384,32]{0,1:T(8,128)(2,1)S(1)}) all-reduce(f32[384,32]{0,1:T(8,128)S(1)} %convolution_bitcast_fusion.1, f32[384,32]{0,1:T(8,128)S(1)} %convolution_bitcast_fusion), channel_id=1, replica_groups=mesh['groups'=2,'dp'=4,'fsdp'=2,'adapter'=2] {'fsdp','adapter'}, use_global_device_ids=true, to_apply=%region_3.4 | all-reduce | flops 24576 | bytes 147456 | tf_op jit(solution)/shard_map/psum | solution.py:73
  65.7 0.2 fusion.5
  65.9 0.3 copy.42
  66.2 0.5 reshape.101
  66.7 0.3 fusion.3
  67.1 0.8 reduce.4
  67.9 0.8 reshape.110
  68.7 3.4 all-to-all-start.3
  72.1 0.4 fusion.4
  72.5 0.1 reshape.103
  72.6 0.4 fusion.1
  73.0 1.0 reduce.5
  74.0 1.0 reshape.112
  75.0 16.2 %all-to-all-done.3 = bf16[4,2,8192]{2,1,0:T(2,128)(2,1)S(1)} async-done(((bf16[4,2,8192]{2,1,0:T(2,128)(2,1)}), bf16[4,2,8192]{2,1,0:T(2,128)(2,1)S(1)}, u32[]{:S(2)}, u32[]{:S(2)}) %all-to-all-start.3) | async-done | bytes 131104 | tf_op jit(solution)/shard_map/all_to_all | solution.py:113
  91.2 4.2 %all-to-all-start.4 = ((bf16[4,2,16384]{2,1,0:T(2,128)(2,1)}), bf16[4,2,16384]{2,1,0:T(2,128)(2,1)}, u32[]{:S(2)}, u32[]{:S(2)}) async-start(bf16[4,2,16384]{2,1,0:T(2,128)(2,1)} %reshape.112), calls=%async_computation.4 | async-start | bytes 524288 | tf_op jit(solution)/shard_map/all_to_all | solution.py:114
  95.4 0.4 fusion.27
  95.8 0.8 reshape.111
  96.6 1.5 convolution_convert_fusion.4
  98.1 3.2 copy.44
  101.3 6.0 %copy.46 = bf16[32,1024,16]{1,2,0:T(8,128)(2,1)} copy(bf16[32,1024,16]{0,2,1:T(8,128)(2,1)} %bitcast.60) | data formatting | bytes 2097152
  107.3 10.5 %all-to-all-done.4 = bf16[4,2,16384]{2,1,0:T(2,128)(2,1)} async-done(((bf16[4,2,16384]{2,1,0:T(2,128)(2,1)}), bf16[4,2,16384]{2,1,0:T(2,128)(2,1)}, u32[]{:S(2)}, u32[]{:S(2)}) %all-to-all-start.4) | async-done | bytes 262176 | tf_op jit(solution)/shard_map/all_to_all | solution.py:114
  117.9 1.2 reshape.113
  119.1 0.8 convolution_convert_fusion
  119.9 2.5 copy.52
  122.4 232.4 %all-gather.5.cloned.1.call-done = bf16[1024,8192]{1,0:T(8,128)(2,1)} async-done(((bf16[1024,2048]{1,0:T(8,128)(2,1)}), bf16[1024,8192]{1,0:T(8,128)(2,1)}) %all-gather.5.cloned.1.call-update) | async-done | bytes 16777232 | tf_op jit(solution)/shard_map/all_gather | solution.py:79
  354.8 12.8 %add_convert_fusion = bf16[384,1024]{1,0:T(8,128)(2,1)} fusion(f32[384,1024]{1,0:T(8,128)S(1)} %fusion.27, bf16[384,8192]{1,0:T(8,128)(2,1)} %all-gather.3.cloned.1.call-done, bf16[1024,8192]{1,0:T(8,128)(2,1)} %all-gather.5.cloned.1.call-done), kind=kOutput, calls=%fused_computation.14 | convolution fusion | flops 6443630592 | bytes 25427968 | tf_op jit(solution)/shard_map/dot_general | solution.py:77
  (10 shorter events, 0.1 us)
Async XLA Ops:
  7.2 40.3 %copy-start = (bf16[384,1024]{1,0:T(8,128)(2,1)S(1)}, bf16[384,1024]{1,0:T(8,128)(2,1)}, u32[]{:S(2)}) copy-start(bf16[384,1024]{1,0:T(8,128)(2,1)} %param.9) | copy-start | bytes 2359300
  7.2 115.2 %all-gather.3.cloned.1.call-start = ((), (), s32[]{:S(2)}) async-start(), calls=%async_computation.5 | async-start | bytes 7864320 | tf_op jit(solution)/shard_map/all_gather | solution.py:76
  7.9 0.8 copy-start.3
  7.9 0.8 copy-start.4
  7.9 346.8 %all-gather.5.cloned.1.call-start = ((), (), s32[]{:S(2)}) async-start(), calls=%async_computation.6 | async-start | bytes 20971520 | tf_op jit(solution)/shard_map/all_gather | solution.py:79
  9.7 16.6 %all-to-all-start = ((s32[4,1,1]{2,1,0:T(1,128)}), s32[4,1,1]{2,1,0:T(1,128)S(1)}, u32[]{:S(2)}, u32[]{:S(2)}) async-start(s32[4,1,1]{2,1,0:T(1,128)} %copy.37), calls=%async_computation | async-start | bytes 4096 | tf_op jit(solution)/shard_map/all_to_all | solution.py:33
  18.7 7.4 %copy-start.2 = (s32[2]{0:T(128)S(1)}, s32[2]{0:T(128)}, u32[]{:S(2)}) copy-start(s32[2]{0:T(128)} %param.14) | copy-start | bytes 28
  32.0 11.0 %all-to-all-start.2 = ((bf16[4,2,8192]{2,1,0:T(2,128)(2,1)}), bf16[4,2,8192]{2,1,0:T(2,128)(2,1)S(1)}, u32[]{:S(2)}, u32[]{:S(2)}) async-start(bf16[4,2,8192]{2,1,0:T(2,128)(2,1)} %reshape.108), calls=%async_computation.2 | async-start | bytes 262144 | tf_op jit(solution)/shard_map/all_to_all | solution.py:48
  43.0 10.2 %all-to-all-start.1 = ((bf16[4,2,16384]{2,1,0:T(2,128)(2,1)}), bf16[4,2,16384]{2,1,0:T(2,128)(2,1)S(1)}, u32[]{:S(2)}, u32[]{:S(2)}) async-start(bf16[4,2,16384]{2,1,0:T(2,128)(2,1)} %reshape.106), calls=%async_computation.1 | async-start | bytes 524288 | tf_op jit(solution)/shard_map/all_to_all | solution.py:49
  46.5 7.4 %copy-start.1 = (bf16[384,2048]{1,0:T(8,128)(2,1)S(1)}, bf16[384,2048]{1,0:T(8,128)(2,1)}, u32[]{:S(2)}) copy-start(bf16[384,2048]{1,0:T(8,128)(2,1)} %param.8) | copy-start | bytes 4718596
  68.7 22.5 %all-to-all-start.3 = ((bf16[4,2,8192]{2,1,0:T(2,128)(2,1)}), bf16[4,2,8192]{2,1,0:T(2,128)(2,1)S(1)}, u32[]{:S(2)}, u32[]{:S(2)}) async-start(bf16[4,2,8192]{2,1,0:T(2,128)(2,1)} %reshape.110), calls=%async_computation.3 | async-start | bytes 262144 | tf_op jit(solution)/shard_map/all_to_all | solution.py:113
  91.2 26.7 %all-to-all-start.4 = ((bf16[4,2,16384]{2,1,0:T(2,128)(2,1)}), bf16[4,2,16384]{2,1,0:T(2,128)(2,1)}, u32[]{:S(2)}, u32[]{:S(2)}) async-start(bf16[4,2,16384]{2,1,0:T(2,128)(2,1)} %reshape.112), calls=%async_computation.4 | async-start | bytes 524288 | tf_op jit(solution)/shard_map/all_to_all | solution.py:114
Sparse Core Ops, SparseCore 0:
  9.6 49.0 all-gather.2
  60.3 294.4 all-gather.4
where the time goes:
time: 375 us; the launch traced here: 374 us
  waiting for transfers between devices  269 us (72%)
  local copies, waits for them, and re-layouts  30.6 us (8%)
  starting transfers between devices  22.6 us (6%)
  matrix products  22.4 us (6%)
  between operations  14.3 us (4%)
  blocking collectives  11.1 us (3%)
  other arithmetic  4.1 us (1%)
    all_gather x1, waiting for transfers between devices, local(): lax.all_gather(frozen_weight, 'dp', axis=1, tiled=True)  232 us
    unnamed x22, local copies, waits for them, and re-layouts  24.7 us
    all_to_all x1, waiting for transfers between devices, local(): lax.all_to_all(out_a, 'dp', split_axis=0, concat_axis=0, tiled=True)  16.2 us
    dot_general x1, matrix products, local(): lax.dot_general(whole_grad, lax.all_gather(frozen_weight, 'dp', axis=1, t...  12.8 us
    psum x1, blocking collectives, local(): up_proj, down_proj = lax.psum((up_part, down_part), ('fsdp', 'adapter'))  11.1 us
    all_to_all x1, waiting for transfers between devices, local(): lax.all_to_all(out_b, 'dp', split_axis=0, concat_axis=0, tiled=True)  10.5 us
  transfers between devices with their start and end apart: 7, of which 5 were waited for; matrix products, arithmetic and copies ran while one was open for 12% of the time, Pallas kernels for 0%

commit v1 on v0

--- a/solution.py
+++ b/solution.py
@@ -73,13 +73,23 @@
     up_proj, down_proj = lax.psum((up_part, down_part), ("fsdp", "adapter"))
     up_factor_block = jnp.where(member_cols, up_proj, 0.0).astype(brain_float_half)
     down_factor_block = jnp.where(member_cols, down_proj, 0.0).astype(brain_float_half)
-    whole_grad = lax.all_gather(output_gradient, ("fsdp", "adapter"), axis=1, tiled=True)
-    frozen_output = lax.dot_general(
-        whole_grad,
-        lax.all_gather(frozen_weight, "dp", axis=1, tiled=True),
-        (((1,), (1,)), ((), ())),
-        preferred_element_type=jnp.float32,
+    n_feat = lax.axis_size(("fsdp", "adapter"))
+    part_rows = tok_rows // n_feat
+    row_part = lax.all_to_all(
+        output_gradient, ("fsdp", "adapter"), split_axis=0, concat_axis=1, tiled=True
     )
+    row_part = lax.all_to_all(row_part, "dp", split_axis=1, concat_axis=0, tiled=True)
+    all_rows = lax.all_gather(row_part, ("fsdp", "adapter"), axis=0, tiled=True)
+    partial_output = lax.dot_general(
+        all_rows, frozen_weight, (((1,), (1,)), ((), ())), preferred_element_type=jnp.float32
+    ).astype(brain_float_half)
+    partial_output = jnp.transpose(
+        partial_output.reshape(n_feat, n_dp, part_rows, features_local), (1, 0, 2, 3)
+    ).reshape(n_dp * tok_rows, features_local)
+    partial_output = lax.all_to_all(
+        partial_output, "dp", split_axis=0, concat_axis=0, tiled=True
+    ).reshape(n_dp, tok_rows, features_local)
+    frozen_output = jnp.sum(partial_output.astype(jnp.float32), axis=0)
     adapter_extra = lax.dot_general(
         up_factor_block, stacked_a, (((1,), (1,)), ((), ())), preferred_element_type=jnp.float32
     )

time: 375 us -> 242 us (0.65)
  waiting for transfers between devices: 269 us -> 67.4 us
  blocking collectives: 11.1 us -> 78.2 us
    all_gather x2 -> x1, waiting for transfers between devices: 232 us -> 0.02 us  [local(): all_rows = lax.all_gather(row_part, ('fsdp', 'adapter'), axis=0, tiled=True)]
    all_to_all x0 -> x2, blocking collectives: none -> 66.7 us  [the longest x1 42.3 us: local(): lax.all_to_all(row_part, 'dp', split_axis=1, concat_axis=0, tiled=True)]
    all_to_all x0 -> x1, waiting for transfers between devices: none -> 55.5 us  [local(): lax.all_to_all(partial_output, 'dp', split_axis=0, concat_axis=0, tiled=T...]
    all_to_all x1, waiting for transfers between devices: 16.2 us -> 3.05 us  [local(): lax.all_to_all(out_a, 'dp', split_axis=0, concat_axis=0, tiled=True)]
    all_to_all x1, waiting for transfers between devices: 10.5 us -> 0.01 us  [local(): lax.all_to_all(out_b, 'dp', split_axis=0, concat_axis=0, tiled=True)]
    all_to_all x0 -> x1, starting transfers between devices: none -> 4.84 us  [local(): lax.all_to_all(partial_output, 'dp', split_axis=0, concat_axis=0, tiled=T...]
  transfers between devices with their start and end apart: 7 -> 7, of which waited for: 5 -> 4; matrix products, arithmetic and copies ran while one was open for 12% -> 22% of each run, Pallas kernels for 0% -> 0%
where the time goes in v1:
time: 242 us; the launch traced here: 241 us
  blocking collectives  78.2 us (32%)
  waiting for transfers between devices  67.4 us (28%)
  local copies, waits for them, and re-layouts  31.3 us (13%)
  starting transfers between devices  23.6 us (10%)
  matrix products  19.6 us (8%)
  between operations  14.3 us (6%)
  other arithmetic  6.82 us (3%)
    all_to_all x1, waiting for transfers between devices, local(): lax.all_to_all(partial_output, 'dp', split_axis=0, concat_axis=0, tiled=T...  55.5 us
    all_to_all x1, blocking collectives, local(): lax.all_to_all(row_part, 'dp', split_axis=1, concat_axis=0, tiled=True)  42.3 us
    all_to_all x1, blocking collectives, local(): lax.all_to_all(output_gradient, ('fsdp', 'adapter'), split_axis=0, concat...  24.4 us
    unnamed x22, local copies, waits for them, and re-layouts  23.3 us
    psum x1, blocking collectives, local(): up_proj, down_proj = lax.psum((up_part, down_part), ('fsdp', 'adapter'))  11.5 us
    dot_general x1, matrix products, local(): lax.dot_general(all_rows, frozen_weight, (((1,), (1,)), ((), ())), prefer...  10.1 us
    all_to_all x1, waiting for transfers between devices, local(): lax.all_to_all(send_b, 'dp', split_axis=0, concat_axis=0, tiled=True)  5.39 us
    all_to_all x1, starting transfers between devices, local(): lax.all_to_all(send_a, 'dp', split_axis=0, concat_axis=0, tiled=True)  5.04 us
  transfers between devices with their start and end apart: 7, of which 4 were waited for; matrix products, arithmetic and copies ran while one was open for 22% of the time, Pallas kernels for 0%

profile of v1, /device:TPU:0, one launch (start us, length us, event | category | flops | bytes accessed | tf_op | source)
XLA Modules:
  0.0 241.2 jit_solution(2016238505907793088)
XLA Ops:
  7.2 0.0 copy-start
  7.2 0.0 all-gather.2.cloned.1.call-start
  7.2 24.4 %all_to_all.98 = bf16[4,96,2048]{2,1,0:T(8,128)(2,1)S(1)} all-to-all(bf16[4,96,2048]{2,1,0:T(8,128)(2,1)} %bitcast.71), channel_id=1, replica_groups=mesh['groups'=2,'dp'=4,'fsdp'=2,'adapter'=2] {'fsdp','adapter'}, dimensions={0} | all-to-all | bytes 3145728 | tf_op jit(solution)/shard_map/all_to_all | solution.py:78
  31.7 42.3 %all_to_all.99 = bf16[96,4,2048]{2,0,1:T(8,128)(2,1)} all-to-all(bf16[96,4,2048]{2,0,1:T(8,128)(2,1)S(1)} %bitcast.76), channel_id=1, replica_groups=mesh['groups'=2,'dp'=4,'fsdp'=2,'adapter'=2] {'dp'}, dimensions={1} | all-to-all | bytes 3145728 | tf_op jit(solution)/shard_map/all_to_all | solution.py:81
  73.9 0.0 all-gather.2.cloned.1.call-update
  74.0 0.2 fusion.17
  74.2 0.1 select_reduce_fusion
  74.3 0.7 copy.41
  74.9 3.2 %all-to-all-start.3 = ((s32[4,1,1]{2,1,0:T(1,128)}), s32[4,1,1]{2,1,0:T(1,128)S(1)}, u32[]{:S(2)}, u32[]{:S(2)}) async-start(s32[4,1,1]{2,1,0:T(1,128)} %copy.41), calls=%async_computation.3 | async-start | bytes 4096 | tf_op jit(solution)/shard_map/all_to_all | solution.py:33
  78.2 3.0 %copy.55 = bf16[4,8,16,2048]{3,1,2,0:T(8,128)(2,1)S(1)} copy(bf16[4,8,16,2048]{3,2,1,0:T(8,128)(2,1)} %bitcast.80) | data formatting | bytes 4194304
  81.1 0.0 copy-start.2
  81.1 7.4 %copy.43 = bf16[32,1024,16]{0,2,1:T(8,128)(2,1)} copy(bf16[32,1024,16]{1,2,0:T(8,128)(2,1)} %param.11) | data formatting | bytes 2097152 | tf_op args[3]
  88.6 0.1 fusion.16
  88.7 0.2 add_reduce_fusion
  88.8 3.4 %fusion.2 = bf16[4,1,16384]{2,0,1:T(4,128)(2,1)S(1)} fusion(bf16[32,16384]{0,1:T(8,128)(2,1)} %bitcast.70, s32[4]{0:T(128)S(1)} %add_reduce_fusion), kind=kOutput, calls=%fused_computation.9 | convolution fusion | flops 4259968 | bytes 1179664 | tf_op jit(solution)/shard_map/dot_general | solution.py:37
  92.2 0.5 broadcast.109
  92.8 0.8 reduce.3
  93.6 0.8 reshape.125
  94.4 5.0 %all-to-all-start.5 = ((bf16[4,2,8192]{2,1,0:T(2,128)(2,1)}), bf16[4,2,8192]{2,1,0:T(2,128)(2,1)S(1)}, u32[]{:S(2)}, u32[]{:S(2)}) async-start(bf16[4,2,8192]{2,1,0:T(2,128)(2,1)} %reshape.125), calls=%async_computation.5 | async-start | bytes 262144 | tf_op jit(solution)/shard_map/all_to_all | solution.py:48
  99.4 0.5 fusion
  99.9 1.0 reduce.2
  100.9 1.0 reshape.123
  101.9 3.5 %all-to-all-done.5 = bf16[4,2,8192]{2,1,0:T(2,128)(2,1)S(1)} async-done(((bf16[4,2,8192]{2,1,0:T(2,128)(2,1)}), bf16[4,2,8192]{2,1,0:T(2,128)(2,1)S(1)}, u32[]{:S(2)}, u32[]{:S(2)}) %all-to-all-start.5) | async-done | bytes 131104 | tf_op jit(solution)/shard_map/all_to_all | solution.py:48
  105.3 3.4 %all-to-all-start.4 = ((bf16[4,2,16384]{2,1,0:T(2,128)(2,1)}), bf16[4,2,16384]{2,1,0:T(2,128)(2,1)S(1)}, u32[]{:S(2)}, u32[]{:S(2)}) async-start(bf16[4,2,16384]{2,1,0:T(2,128)(2,1)} %reshape.123), calls=%async_computation.4 | async-start | bytes 524288 | tf_op jit(solution)/shard_map/all_to_all | solution.py:49
  108.8 0.1 reshape.126
  108.9 0.0 copy-start.1
  108.9 0.3 convolution_convert_fusion.7
  109.2 0.4 reshape.115
  109.6 0.2 copy.45
  109.8 0.3 convolution_bitcast_fusion
  110.1 5.4 %all-to-all-done.4 = bf16[4,2,16384]{2,1,0:T(2,128)(2,1)S(1)} async-done(((bf16[4,2,16384]{2,1,0:T(2,128)(2,1)}), bf16[4,2,16384]{2,1,0:T(2,128)(2,1)S(1)}, u32[]{:S(2)}, u32[]{:S(2)}) %all-to-all-start.4) | async-done | bytes 262176 | tf_op jit(solution)/shard_map/all_to_all | solution.py:49
  115.5 0.3 reshape.124
  115.8 0.4 convolution_convert_fusion.3
  116.2 0.1 reshape.113
  116.3 0.6 convolution_bitcast_fusion.1
  116.9 11.5 %all-reduce = (bf16[384,32]{0,1:T(8,128)(2,1)S(1)}, bf16[384,32]{0,1:T(8,128)(2,1)S(1)}) all-reduce(f32[384,32]{0,1:T(8,128)S(1)} %convolution_bitcast_fusion.1, f32[384,32]{0,1:T(8,128)S(1)} %convolution_bitcast_fusion), channel_id=1, replica_groups=mesh['groups'=2,'dp'=4,'fsdp'=2,'adapter'=2] {'fsdp','adapter'}, use_global_device_ids=true, to_apply=%region_4.5 | all-reduce | flops 24576 | bytes 147456 | tf_op jit(solution)/shard_map/psum | solution.py:73
  128.4 0.2 fusion.5
  128.7 0.3 copy.46
  128.9 0.5 reshape.118
  129.5 0.3 fusion.3
  129.8 0.8 reduce.4
  130.6 0.8 reshape.127
  131.4 3.4 %all-to-all-start.6 = ((bf16[4,2,8192]{2,1,0:T(2,128)(2,1)}), bf16[4,2,8192]{2,1,0:T(2,128)(2,1)S(1)}, u32[]{:S(2)}, u32[]{:S(2)}) async-start(bf16[4,2,8192]{2,1,0:T(2,128)(2,1)} %reshape.127), calls=%async_computation.6 | async-start | bytes 262144 | tf_op jit(solution)/shard_map/all_to_all | solution.py:123
  134.9 0.4 fusion.4
  135.3 0.1 reshape.120
  135.4 0.4 fusion.1
  135.8 1.0 reduce.5
  136.8 1.0 reshape.129
  137.8 3.1 %all-to-all-done.6 = bf16[4,2,8192]{2,1,0:T(2,128)(2,1)S(1)} async-done(((bf16[4,2,8192]{2,1,0:T(2,128)(2,1)}), bf16[4,2,8192]{2,1,0:T(2,128)(2,1)S(1)}, u32[]{:S(2)}, u32[]{:S(2)}) %all-to-all-start.6) | async-done | bytes 131104 | tf_op jit(solution)/shard_map/all_to_all | solution.py:123
  140.8 3.6 %all-to-all-start.7 = ((bf16[4,2,16384]{2,1,0:T(2,128)(2,1)}), bf16[4,2,16384]{2,1,0:T(2,128)(2,1)S(1)}, u32[]{:S(2)}, u32[]{:S(2)}) async-start(bf16[4,2,16384]{2,1,0:T(2,128)(2,1)} %reshape.129), calls=%async_computation.7 | async-start | bytes 524288 | tf_op jit(solution)/shard_map/all_to_all | solution.py:124
  144.4 0.0 all-gather.2.cloned.1.call-done
  144.4 10.1 %convolution_convert_fusion.8 = bf16[1536,1024]{1,0:T(8,128)(2,1)S(1)} fusion(bf16[1536,2048]{1,0:T(8,128)(2,1)} %all-gather.2.cloned.1.call-done, bf16[1024,2048]{1,0:T(8,128)(2,1)} %param.10), kind=kOutput, calls=%fused_computation.13 | convolution fusion | flops 6444023808 | bytes 13631488 | tf_op jit(solution)/shard_map/dot_general | solution.py:83
  154.5 2.1 copy.40
  156.6 4.8 %all-to-all-start.2 = ((bf16[4,384,1024]{2,1,0:T(8,128)(2,1)}), bf16[4,384,1024]{2,1,0:T(8,128)(2,1)}, u32[]{:S(2)}, u32[]{:S(2)}) async-start(bf16[4,384,1024]{2,1,0:T(8,128)(2,1)} %bitcast.72), calls=%async_computation.2 | async-start | bytes 6291456 | tf_op jit(solution)/shard_map/all_to_all | solution.py:89
  161.4 0.1 reshape.128
  161.5 0.6 convolution_convert_fusion.4
  162.1 3.1 %copy.48 = bf16[32,16384]{0,1:T(8,128)(2,1)} copy(bf16[32,16384]{1,0:T(8,128)(2,1)S(1)} %convolution_convert_fusion.4) | data formatting | bytes 2097152 | tf_op jit(solution)/shard_map/convert_element_type | solution.py:129
  165.3 6.0 %copy.50 = bf16[32,1024,16]{1,2,0:T(8,128)(2,1)} copy(bf16[32,1024,16]{0,2,1:T(8,128)(2,1)} %bitcast.69) | data formatting | bytes 2097152
  171.3 0.3 reshape.130
  171.6 0.8 convolution_convert_fusion
  172.4 2.5 %copy.56 = bf16[4,8,16,2048]{3,2,1,0:T(8,128)(2,1)} copy(bf16[4,8,16,2048]{3,1,2,0:T(8,128)(2,1)S(1)} %bitcast.74) | data formatting | bytes 4194304
  174.9 55.5 %all-to-all-done.2 = bf16[4,384,1024]{2,1,0:T(8,128)(2,1)} async-done(((bf16[4,384,1024]{2,1,0:T(8,128)(2,1)}), bf16[4,384,1024]{2,1,0:T(8,128)(2,1)}, u32[]{:S(2)}, u32[]{:S(2)}) %all-to-all-start.2) | async-done | bytes 3145760 | tf_op jit(solution)/shard_map/all_to_all | solution.py:89
  230.3 2.7 %convert_reduce_fusion = f32[384,1024]{1,0:T(8,128)S(1)} fusion(bf16[4,384,1024]{2,1,0:T(8,128)(2,1)} %all-to-all-done.2), kind=kLoop, calls=%fused_computation.12 | loop fusion | flops 2752512 | bytes 4718592 | tf_op jit(solution)/shard_map/reduce_sum | solution.py:92
  233.1 1.3 add_convert_fusion
  (13 shorter events, 0.1 us)
Async XLA Ops:
  7.2 102.6 %copy-start = (bf16[384,1024]{1,0:T(8,128)(2,1)S(1)}, bf16[384,1024]{1,0:T(8,128)(2,1)}, u32[]{:S(2)}) copy-start(bf16[384,1024]{1,0:T(8,128)(2,1)} %param.9) | copy-start | bytes 2359300
  7.2 137.2 %all-gather.2.cloned.1.call-start = ((), (), s32[]{:S(2)}) async-start(), calls=%async_computation.8 | async-start | bytes 7864320 | tf_op jit(solution)/shard_map/all_gather | solution.py:82
  31.7 42.3 %copy-start.3 = (s32[128]{0:T(128)S(1)}, s32[128]{0:T(128)}, u32[]{:S(2)}) copy-start(s32[128]{0:T(128)} %param.15) | copy-start | bytes 1540
  31.7 42.3 %copy-start.4 = (s32[2]{0:T(128)S(1)}, s32[2]{0:T(128)}, u32[]{:S(2)}) copy-start(s32[2]{0:T(128)} %param.13) | copy-start | bytes 28
  74.9 13.7 %all-to-all-start.3 = ((s32[4,1,1]{2,1,0:T(1,128)}), s32[4,1,1]{2,1,0:T(1,128)S(1)}, u32[]{:S(2)}, u32[]{:S(2)}) async-start(s32[4,1,1]{2,1,0:T(1,128)} %copy.41), calls=%async_computation.3 | async-start | bytes 4096 | tf_op jit(solution)/shard_map/all_to_all | solution.py:33
  81.1 7.4 %copy-start.2 = (s32[2]{0:T(128)S(1)}, s32[2]{0:T(128)}, u32[]{:S(2)}) copy-start(s32[2]{0:T(128)} %param.14) | copy-start | bytes 28
  94.4 11.0 %all-to-all-start.5 = ((bf16[4,2,8192]{2,1,0:T(2,128)(2,1)}), bf16[4,2,8192]{2,1,0:T(2,128)(2,1)S(1)}, u32[]{:S(2)}, u32[]{:S(2)}) async-start(bf16[4,2,8192]{2,1,0:T(2,128)(2,1)} %reshape.125), calls=%async_computation.5 | async-start | bytes 262144 | tf_op jit(solution)/shard_map/all_to_all | solution.py:48
  105.3 10.2 %all-to-all-start.4 = ((bf16[4,2,16384]{2,1,0:T(2,128)(2,1)}), bf16[4,2,16384]{2,1,0:T(2,128)(2,1)S(1)}, u32[]{:S(2)}, u32[]{:S(2)}) async-start(bf16[4,2,16384]{2,1,0:T(2,128)(2,1)} %reshape.123), calls=%async_computation.4 | async-start | bytes 524288 | tf_op jit(solution)/shard_map/all_to_all | solution.py:49
  108.9 7.4 %copy-start.1 = (bf16[384,2048]{1,0:T(8,128)(2,1)S(1)}, bf16[384,2048]{1,0:T(8,128)(2,1)}, u32[]{:S(2)}) copy-start(bf16[384,2048]{1,0:T(8,128)(2,1)} %param.8) | copy-start | bytes 4718596
  131.4 9.4 %all-to-all-start.6 = ((bf16[4,2,8192]{2,1,0:T(2,128)(2,1)}), bf16[4,2,8192]{2,1,0:T(2,128)(2,1)S(1)}, u32[]{:S(2)}, u32[]{:S(2)}) async-start(bf16[4,2,8192]{2,1,0:T(2,128)(2,1)} %reshape.127), calls=%async_computation.6 | async-start | bytes 262144 | tf_op jit(solution)/shard_map/all_to_all | solution.py:123
  140.8 15.8 %all-to-all-start.7 = ((bf16[4,2,16384]{2,1,0:T(2,128)(2,1)}), bf16[4,2,16384]{2,1,0:T(2,128)(2,1)S(1)}, u32[]{:S(2)}, u32[]{:S(2)}) async-start(bf16[4,2,16384]{2,1,0:T(2,128)(2,1)} %reshape.129), calls=%async_computation.7 | async-start | bytes 524288 | tf_op jit(solution)/shard_map/all_to_all | solution.py:124
  156.6 73.8 %all-to-all-start.2 = ((bf16[4,384,1024]{2,1,0:T(8,128)(2,1)}), bf16[4,384,1024]{2,1,0:T(8,128)(2,1)}, u32[]{:S(2)}, u32[]{:S(2)}) async-start(bf16[4,384,1024]{2,1,0:T(8,128)(2,1)} %bitcast.72), calls=%async_computation.2 | async-start | bytes 6291456 | tf_op jit(solution)/shard_map/all_to_all | solution.py:89
Sparse Core Ops, SparseCore 0:
  74.1 44.8 all-gather.1

commit v2 on v0

v2 whole, which is shorter than its diff:
```python
import functools

import jax
import jax.numpy as jnp
from jax import lax
from jax.experimental import pallas as pl
from jax.experimental.pallas import tpu as pltpu
from jax.sharding import PartitionSpec as P

adapter_scale = 2.0
float_half = jnp.bfloat16
both_minor = (((1,), (1,)), ((), ()))
both_major = (((0,), (0,)), ((), ()))


def flip(index, step):
    out, bit = index, 1
    while bit <= step:
        if step & bit:
            out = out + bit - 2 * bit * ((index // bit) % 2)
        bit *= 2
    return out


def copy_to(src, dst, send_sem, recv_sem, device):
    return pltpu.make_async_remote_copy(
        src_ref=src,
        dst_ref=dst,
        send_sem=send_sem,
        recv_sem=recv_sem,
        device_id=device,
        device_id_type=pl.DeviceIdType.MESH,
    )


def kernel(
    n_dp,
    n_fsdp,
    n_core,
    rank,
    grad_ref,
    act_ref,
    weight_hbm,
    down_hbm,
    up_hbm,
    asked_ref,
    key_ref,
    mask_ref,
    out_ref,
    back_ref,
    sel_ref,
    weight,
    down,
    up,
    asked_in,
    factor_out,
    factor_in,
    proj_out,
    proj_in,
    back_out,
    back_in,
    rows_in,
    grad_all,
    part_out,
    part_in,
    total,
    load_sem,
    asked_s,
    asked_r,
    factor_s,
    factor_r,
    proj_s,
    proj_r,
    back_s,
    back_r,
    rows_s,
    rows_r,
    grad_s,
    grad_r,
    cross_s,
    cross_r,
    core_s,
    core_r,
    part_s,
    part_r,
):
    dp, fsdp, core = lax.axis_index("dp"), lax.axis_index("fsdp"), lax.axis_index("adapter")
    feat = fsdp * n_core + core
    n_feat = n_fsdp * n_core
    tok, width = grad_ref.shape
    feats = act_ref.shape[1]
    rows = tok // n_feat
    width_dp = grad_all.shape[2]
    per_feat = n_dp // n_feat

    def feat_device(index):
        return {"fsdp": index // n_core, "adapter": index % n_core}

    def rank_rows(index):
        return pl.ds(pl.multiple_of(index * rank, rank), rank)

    def token_rows(index):
        return pl.ds(pl.multiple_of(index * rows, rows), rows)

    loads = [
        pltpu.make_async_copy(src, dst, load_sem.at[i])
        for i, (src, dst) in enumerate(((down_hbm, down), (up_hbm, up), (weight_hbm, weight)))
    ]
    for load in loads:
        load.start()

    barrier = pltpu.get_barrier_semaphore()
    for step in range(1, n_dp):
        pl.semaphore_signal(
            barrier,
            inc=1,
            device_id={"dp": flip(dp, step)},
            device_id_type=pl.DeviceIdType.MESH,
        )
    for step in range(1, n_feat):
        pl.semaphore_signal(
            barrier,
            inc=1,
            device_id=feat_device(flip(feat, step)),
            device_id_type=pl.DeviceIdType.MESH,
        )
    pl.semaphore_wait(barrier, n_dp + n_feat - 2)

    def dp_exchange(step, src, dst, send, recv):
        peer = flip(dp, step)
        return copy_to(
            src.at[rank_rows(peer)],
            dst.at[rank_rows(dp)],
            send.at[peer],
            recv.at[dp],
            {"dp": peer},
        )

    def dp_arrival(step, src, dst, send, recv):
        peer = flip(dp, step)
        return copy_to(
            src.at[rank_rows(peer)],
            dst.at[rank_rows(peer)],
            send.at[peer],
            recv.at[peer],
            {"dp": peer},
        )

    asked_args = (asked_ref, asked_in, asked_s, asked_r)
    factor_args = (factor_out, factor_in, factor_s, factor_r)
    back_args = (back_out, back_in, back_s, back_r)

    for step in range(1, n_dp):
        dp_exchange(step, *asked_args).start()
    asked_in[rank_rows(dp), :] = asked_ref[rank_rows(dp), :]

    def rows_copy(step):
        peer = flip(feat, step)
        return copy_to(
            grad_ref.at[token_rows(peer)],
            rows_in.at[feat],
            rows_s.at[peer],
            rows_r.at[feat],
            feat_device(peer),
        )

    def rows_arrival(step):
        peer = flip(feat, step)
        return copy_to(
            grad_ref.at[token_rows(peer)],
            rows_in.at[peer],
            rows_s.at[peer],
            rows_r.at[peer],
            feat_device(peer),
        )

    for step in range(1, n_feat):
        rows_copy(step).start()

    def grad_copy(step, part):
        source = flip(feat, step)
        target = source * per_feat + part
        columns = pl.ds(part * width_dp, width_dp)
        if step == 0:
            block = grad_ref.at[token_rows(feat), columns]
        else:
            block = rows_in.at[source, :, columns]
        copy = copy_to(
            block,
            grad_all.at[dp, token_rows(feat)],
            grad_s.at[target],
            grad_r.at[dp],
            {"dp": target},
        )
        return target, block, copy

    def forward(step):
        for part in range(per_feat):
            target, block, copy = grad_copy(step, part)

            @pl.when(target != dp)
            def _():
                copy.start()

            @pl.when(target == dp)
            def _():
                grad_all[dp, token_rows(feat), :] = block[...]

    forward(0)

    loads[0].wait()
    loads[1].wait()
    for step in range(1, n_dp):
        dp_arrival(step, *asked_args).wait_recv()
    chosen = jnp.where(asked_in[...] - 1 == key_ref[...], 1.0, 0.0).astype(float_half)
    sel_ref[...] = chosen
    factor_out[:, :feats] = jnp.dot(
        chosen, down[...], preferred_element_type=jnp.float32
    ).astype(float_half)
    factor_out[:, feats:] = jnp.dot(
        chosen, up[...], preferred_element_type=jnp.float32
    ).astype(float_half)
    for step in range(1, n_dp):
        dp_exchange(step, *factor_args).start()
    factor_in[rank_rows(dp), :] = factor_out[rank_rows(dp), :]

    for step in range(1, n_feat):
        rows_arrival(step).wait_recv()
        forward(step)

    def proj_copy(step):
        peer = flip(feat, step)
        return copy_to(
            proj_out, proj_in.at[feat], proj_s.at[peer], proj_r.at[feat], feat_device(peer)
        )

    def proj_arrival(step):
        peer = flip(feat, step)
        return copy_to(
            proj_out, proj_in.at[peer], proj_s.at[peer], proj_r.at[peer], feat_device(peer)
        )

    def in_owner(owner):
        return mask_ref[owner : owner + 1, :] > 0.0

    def project():
        for step in range(1, n_dp):
            dp_arrival(step, *factor_args).wait_recv()
        for half, (factor, value) in enumerate(
            ((factor_in[:, feats:], grad_ref[...]), (factor_in[:, :feats], act_ref[...]))
        ):
            product = lax.dot_general(
                factor, value, both_minor, preferred_element_type=jnp.float32
            )
            folded = jnp.zeros((rank, tok), jnp.float32)
            for owner in range(n_dp):
                folded += jnp.where(
                    in_owner(owner), product[owner * rank : (owner + 1) * rank], 0.0
                )
            proj_out[half * rank : (half + 1) * rank, :] = folded
        for step in range(1, n_feat):
            proj_copy(step).start()
        proj_in[feat] = proj_out[...]

    def adapter_gradients():
        for step in range(1, n_feat):
            proj_arrival(step).wait_recv()
        summed = proj_in[0]
        for index in range(1, n_feat):
            summed += proj_in[index]

        def spread(values):
            return jnp.concatenate(
                [jnp.where(in_owner(owner), values, 0.0) for owner in range(n_dp)], axis=0
            ).astype(float_half)

        up_block, down_block = spread(summed[:rank]), spread(summed[rank:])
        back_out[:, :feats] = (
            adapter_scale
            * jnp.dot(up_block, act_ref[...], preferred_element_type=jnp.float32)
        ).astype(float_half)
        back_out[:, feats:] = (
            adapter_scale
            * jnp.dot(down_block, grad_ref[...], preferred_element_type=jnp.float32)
        ).astype(float_half)
        for step in range(1, n_dp):
            dp_exchange(step, *back_args).start()
        back_in[rank_rows(dp), :] = back_out[rank_rows(dp), :]
        total[...] += adapter_scale * lax.dot_general(
            up_block, factor_in[:, :feats], both_major, preferred_element_type=jnp.float32
        )

    def grad_arrival(step):
        peer = flip(dp, step)
        block = grad_all.at[peer, token_rows(feat)]
        return copy_to(block, block, grad_s.at[peer], grad_r.at[peer], {"dp": peer})

    def cross_copy(index, step):
        peer = flip(fsdp, step)
        block = grad_all.at[index, token_rows(feat)]
        return copy_to(
            block, block, cross_s.at[index, peer], cross_r.at[index, fsdp], {"fsdp": peer}
        )

    def cross_arrival(index, step):
        peer = flip(fsdp, step)
        block = grad_all.at[index, token_rows(peer * n_core + core)]
        return copy_to(
            block, block, cross_s.at[index, peer], cross_r.at[index, peer], {"fsdp": peer}
        )

    def core_copy(index, step, side):
        chip, peer = flip(fsdp, step), flip(core, side)
        block = grad_all.at[index, token_rows(chip * n_core + core)]
        return copy_to(
            block,
            block,
            core_s.at[index, chip, peer],
            core_r.at[index, chip, core],
            {"adapter": peer},
        )

    def core_arrival(index, step, side):
        chip, peer = flip(fsdp, step), flip(core, side)
        block = grad_all.at[index, token_rows(chip * n_core + peer)]
        return copy_to(
            block,
            block,
            core_s.at[index, chip, peer],
            core_r.at[index, chip, peer],
            {"adapter": peer},
        )

    def part_copy(step):
        peer = flip(dp, step)
        return copy_to(
            part_out.at[peer], part_in.at[dp], part_s.at[peer], part_r.at[dp], {"dp": peer}
        )

    def part_arrival(step):
        peer = flip(dp, step)
        return copy_to(
            part_out.at[peer], part_in.at[peer], part_s.at[peer], part_r.at[peer], {"dp": peer}
        )

    tile = 256 if feats % 256 == 0 else feats

    def multiply(step):
        index = flip(dp, step)

        def one(i, carry):
            columns = pl.ds(pl.multiple_of(i * tile, tile), tile)
            product = lax.dot_general(
                grad_all[index], weight[columns, :], both_minor, preferred_element_type=jnp.float32
            )
            if step == 0:
                total[:, columns] = product
            else:
                part_out[index, :, columns] = product.astype(float_half)
            return carry

        lax.fori_loop(0, feats // tile, one, 0)
        if step:
            part_copy(step).start()

    for turn in range(n_dp + 2):
        if turn < n_dp:
            if turn:
                grad_arrival(turn).wait_recv()
            index = flip(dp, turn)
            for step in range(1, n_fsdp):
                cross_copy(index, step).start()
            for side in range(1, n_core):
                core_copy(index, 0, side).start()
        if turn == 0:
            project()
            loads[2].wait()
        if 1 <= turn <= n_dp:
            index = flip(dp, turn - 1)
            for step in range(1, n_fsdp):
                cross_arrival(index, step).wait_recv()
                for side in range(1, n_core):
                    core_copy(index, step, side).start()
        if turn >= 2:
            index = flip(dp, turn - 2)
            for step in range(n_fsdp):
                for side in range(1, n_core):
                    core_arrival(index, step, side).wait_recv()
            multiply(turn - 2)
        if turn == 2:
            adapter_gradients()

    for step in range(1, n_dp):
        part_arrival(step).wait_recv()
        total[...] += part_in[flip(dp, step)].astype(jnp.float32)
    out_ref[...] = total[...].astype(float_half)
    for step in range(1, n_dp):
        dp_arrival(step, *back_args).wait_recv()
    back_ref[...] = back_in[...]

    for step in range(1, n_dp):
        for args in (asked_args, factor_args, back_args):
            dp_exchange(step, *args).wait_send()
        part_copy(step).wait_send()
    for step in range(1, n_feat):
        rows_copy(step).wait_send()
        proj_copy(step).wait_send()
    for step in range(n_feat):
        for part in range(per_feat):
            target, _, copy = grad_copy(step, part)

            @pl.when(target != dp)
            def _():
                copy.wait_send()

    for turn in range(n_dp):
        index = flip(dp, turn)
        for step in range(1, n_fsdp):
            cross_copy(index, step).wait_send()
        for step in range(n_fsdp):
            for side in range(1, n_core):
                core_copy(index, step, side).wait_send()


def local(
    output_gradient,
    attention_output,
    frozen_weight,
    adapter_down_table,
    adapter_up_table,
    segment_adapter,
    segment_first_token,
    adapter_table_row,
):
    n_dp, n_fsdp, n_core = (lax.axis_size(name) for name in ("dp", "fsdp", "adapter"))
    n_feat = n_fsdp * n_core
    segs = segment_adapter.shape[0]
    tok, width = output_gradient.shape
    table, feats, rank = adapter_down_table.shape
    width_dp = frozen_weight.shape[1]
    hits = (
        segment_adapter[:, None] == jnp.arange(adapter_table_row.shape[0], dtype=jnp.int32)[None, :]
    )
    table_rows = jnp.sum(jnp.where(hits, adapter_table_row[None, :], 0), axis=1)
    owners = table_rows // table
    to_owner = owners[:, None] == jnp.arange(n_dp, dtype=jnp.int32)[None, :]
    asked = jnp.sum(jnp.where(to_owner, (table_rows % table + 1)[:, None], 0), axis=0)
    asked = jnp.broadcast_to(asked[:, None, None], (n_dp, rank, table * rank)).reshape(
        n_dp * rank, table * rank
    )
    row_of = lax.broadcasted_iota(jnp.int32, (n_dp * rank, table * rank), 0)
    col_of = lax.broadcasted_iota(jnp.int32, (n_dp * rank, table * rank), 1)
    key = jnp.where(row_of % rank == col_of % rank, col_of // rank, -5)
    places = jnp.arange(tok, dtype=jnp.int32)
    seg_of = (
        jnp.sum((places[:, None] >= segment_first_token[None, :]).astype(jnp.int32), axis=1) - 1
    )
    member = seg_of[None, :] == jnp.arange(segs, dtype=jnp.int32)[:, None]
    mask = jnp.sum(
        (to_owner[:, :, None] & member[:, None, :]).astype(jnp.float32), axis=0
    )
    down = jnp.transpose(adapter_down_table, (0, 2, 1)).reshape(table * rank, feats)
    up = adapter_up_table.reshape(table * rank, width)
    both = feats + width
    vmem = pl.BlockSpec(memory_space=pltpu.VMEM)
    hbm = pl.BlockSpec(memory_space=pl.ANY)
    dma = pltpu.SemaphoreType.DMA
    pair = [dma((n_dp,)), dma((n_dp,))]
    feat_pair = [dma((n_feat,)), dma((n_feat,))]
    input_gradient, back, chosen = pl.pallas_call(
        functools.partial(kernel, n_dp, n_fsdp, n_core, rank),
        out_shape=(
            jax.ShapeDtypeStruct((tok, feats), float_half),
            jax.ShapeDtypeStruct((n_dp * rank, both), float_half),
            jax.ShapeDtypeStruct((n_dp * rank, table * rank), float_half),
        ),
        in_specs=[vmem, vmem, hbm, hbm, hbm, vmem, vmem, vmem],
        out_specs=[vmem] * 3,
        scratch_shapes=[
            pltpu.VMEM((feats, width_dp), float_half),
            pltpu.VMEM((table * rank, feats), float_half),
            pltpu.VMEM((table * rank, width), float_half),
            pltpu.VMEM((n_dp * rank, table * rank), jnp.int32),
            pltpu.VMEM((n_dp * rank, both), float_half),
            pltpu.VMEM((n_dp * rank, both), float_half),
            pltpu.VMEM((2 * rank, tok), jnp.float32),
            pltpu.VMEM((n_feat, 2 * rank, tok), jnp.float32),
            pltpu.VMEM((n_dp * rank, both), float_half),
            pltpu.VMEM((n_dp * rank, both), float_half),
            pltpu.VMEM((n_feat, tok // n_feat, width), float_half),
            pltpu.VMEM((n_dp, tok, width_dp), float_half),
            pltpu.VMEM((n_dp, tok, feats), float_half),
            pltpu.VMEM((n_dp, tok, feats), float_half),
            pltpu.VMEM((tok, feats), jnp.float32),
            dma((3,)),
            *pair,
            *pair,
            *feat_pair,
            *pair,
            *feat_pair,
            *pair,
            dma((n_dp, n_fsdp)),
            dma((n_dp, n_fsdp)),
            dma((n_dp, n_fsdp, n_core)),
            dma((n_dp, n_fsdp, n_core)),
            *pair,
        ],
        compiler_params=pltpu.CompilerParams(
            collective_id=0, has_side_effects=True, vmem_limit_bytes=56 * 2**20
        ),
        cost_estimate=pl.CostEstimate(
            flops=2 * n_dp * tok * width_dp * feats,
            bytes_accessed=2 * (feats * width_dp + 2 * tok * (width + feats)),
            transcendentals=0,
        ),
    )(output_gradient, attention_output, frozen_weight, down, up, asked, key, mask)
    grad_a = lax.dot_general(
        chosen, back[:, :feats], both_major, preferred_element_type=jnp.float32
    ).astype(float_half)
    grad_b = lax.dot_general(
        chosen, back[:, feats:], both_major, preferred_element_type=jnp.float32
    ).astype(float_half)
    grad_a = jnp.transpose(grad_a.reshape(table, rank, feats), (0, 2, 1))
    return input_gradient, grad_a, grad_b.reshape(table, rank, width)


def solution(mesh):
    in_specs = (
        P(("groups", "dp"), ("fsdp", "adapter")),
        P(("groups", "dp"), ("fsdp", "adapter")),
        P(("fsdp", "adapter"), "dp"),
        P(("groups", "dp"), ("fsdp", "adapter"), None),
        P(("groups", "dp"), None, ("fsdp", "adapter")),
        P(("groups", "dp")),
        P(("groups", "dp")),
        P("groups"),
    )
    out_specs = (
        P(("groups", "dp"), ("fsdp", "adapter")),
        P(("groups", "dp"), ("fsdp", "adapter"), None),
        P(("groups", "dp"), None, ("fsdp", "adapter")),
    )
    return jax.shard_map(local, mesh=mesh, in_specs=in_specs, out_specs=out_specs, check_vma=False)
```

time: 375 us -> 155 us (0.41)
  the two profiles are of different devices: /device:TPU:0 before, /device:TPU:18 now
where the time goes in v2:
time: 155 us
  Pallas kernels  143 us (92%)
  matrix products  5.47 us (4%)
  other arithmetic  3.23 us (2%)
  local copies, waits for them, and re-layouts  1.77 us (1%)
    pallas_call x1, Pallas kernels, local(): pl.pallas_call(functools.partial(kernel, n_dp, n_fsdp, n_core, rank), out...  143 us

profile of v2, /device:TPU:18, one launch (start us, length us, event | category | flops | bytes accessed | tf_op | source)
XLA Modules:
  0.0 154.5 jit_solution(15523687064920151102)
XLA Ops:
  0.6 0.9 fusion.9
  1.5 0.1 select_reduce_fusion
  1.6 0.1 iota_compare_fusion.1
  1.7 0.1 broadcast_in_dim.54
  1.7 0.1 broadcast_in_dim.55
  1.8 0.7 fusion.2
  2.6 0.7 convert_reduce_fusion.mask_ref
  3.3 0.8 select_select_fusion.key_ref
  4.0 0.7 broadcast_in_dim.56.asked_ref
  4.8 143.4 %shard_map.103 = (bf16[384,1024]{1,0:T(8,128)(2,1)}, bf16[64,3072]{1,0:T(8,128)(2,1)}, bf16[64,512]{1,0:T(8,128)(2,1)}) custom-call(bf16[384,2048]{1,0:T(8,128)(2,1)} %grad_ref.1, bf16[384,1024]{1,0:T(8,128)(2,1)} %act_ref.1, bf16[1024,2048]{1,0:T(8,128)(2,1)} %weight_hbm.1, bf16[512,1024]{1,0:T(8,128)(2,1)} %bitcast.13, bf16[512,2048]{1,0:T(8,128)(2,1)} %bitcast.12, ...), custom_call_target="tpu_custom_call" | custom-call | flops 6442450944 | bytes 8912896 | tf_op jit(solution)/shard_map/pallas_call | solution.py:470
  148.2 0.0 copy-start
  148.2 2.4 %convolution_convert_fusion.1 = bf16[512,1024]{1,0:T(8,128)(2,1)} fusion(bf16[64,512]{1,0:T(8,128)(2,1)} %get-tuple-element.7, bf16[64,3072]{1,0:T(8,128)(2,1)} %get-tuple-element.8), kind=kOutput, calls=%fused_computation.1 | convolution fusion | flops 67633152 | bytes 1245184 | tf_op jit(solution)/shard_map/dot_general | solution.py:517
  150.6 3.0 %convolution_convert_fusion = bf16[512,2048]{1,0:T(8,128)(2,1)} fusion(bf16[64,512]{1,0:T(8,128)(2,1)} %get-tuple-element.7, bf16[64,3072]{1,0:T(8,128)(2,1)} %get-tuple-element.8), kind=kOutput, calls=%fused_computation | convolution fusion | flops 135266304 | bytes 2424832 | tf_op jit(solution)/shard_map/dot_general | solution.py:520
  153.6 0.0 copy-done
  153.6 0.9 copy.12
  (8 shorter events, 0.0 us)
Async XLA Ops:
  148.2 5.5 %copy-start = (bf16[384,1024]{1,0:T(8,128)(2,1)S(1)}, bf16[384,1024]{1,0:T(8,128)(2,1)}, u32[]{:S(2)}) copy-start(bf16[384,1024]{1,0:T(8,128)(2,1)} %get-tuple-element.22) | copy-start | bytes 2359300

commit v3 on v2

--- a/solution.py
+++ b/solution.py
@@ -63,6 +63,7 @@
     grad_all,
     part_out,
     part_in,
+    product,
     total,
     load_sem,
     asked_s,
@@ -290,8 +291,7 @@
             up_block, factor_in[:, :feats], both_major, preferred_element_type=jnp.float32
         )
 
-    def grad_arrival(step):
-        peer = flip(dp, step)
+    def grad_arrival(peer):
         block = grad_all.at[peer, token_rows(feat)]
         return copy_to(block, block, grad_s.at[peer], grad_r.at[peer], {"dp": peer})
 
@@ -331,43 +331,91 @@
             {"adapter": peer},
         )
 
-    def part_copy(step):
-        peer = flip(dp, step)
-        return copy_to(
-            part_out.at[peer], part_in.at[dp], part_s.at[peer], part_r.at[dp], {"dp": peer}
-        )
-
-    def part_arrival(step):
-        peer = flip(dp, step)
-        return copy_to(
-            part_out.at[peer], part_in.at[peer], part_s.at[peer], part_r.at[peer], {"dp": peer}
+    def order(turn):
+        if turn == 0:
+            return dp
+        upper = dp // (n_dp // 2)
+        falling, rising = n_dp - turn, turn - 1
+        falling = falling - (dp - falling + n_dp) // n_dp
+        rising = rising + (rising - dp + n_dp) // n_dp
+        return (1 - upper) * falling + upper * rising
+
+    def part_copy(turn):
+        index = order(turn)
+        above = (index - dp - 1 + n_dp) // n_dp
+        following = dp + 2 * above - 1
+        ends = (1 - above) * (1 - (following - index + n_dp - 1) // n_dp)
+        slot = index + ends * (n_dp - index)
+        return copy_to(
+            part_out.at[index],
+            part_in.at[slot],
+            part_s.at[index],
+            part_r.at[slot],
+            {"dp": following},
+        )
+
+    def part_arrival(slot):
+        return copy_to(
+            part_out.at[0], part_in.at[slot], part_s.at[0], part_r.at[slot], {"dp": flip(dp, 1)}
         )
 
     tile = 256 if feats % 256 == 0 else feats
 
-    def multiply(step):
-        index = flip(dp, step)
-
+    def multiply(index, store):
         def one(i, carry):
             columns = pl.ds(pl.multiple_of(i * tile, tile), tile)
-            product = lax.dot_general(
-                grad_all[index], weight[columns, :], both_minor, preferred_element_type=jnp.float32
+            store(
+                columns,
+                lax.dot_general(
+                    grad_all[index],
+                    weight[columns, :],
+                    both_minor,
+                    preferred_element_type=jnp.float32,
+                ),
             )
-            if step == 0:
-                total[:, columns] = product
-            else:
-                part_out[index, :, columns] = product.astype(float_half)
             return carry
 
         lax.fori_loop(0, feats // tile, one, 0)
-        if step:
-            part_copy(step).start()
+
+    outermost = dp * (n_dp - 1 - dp) == 0
+
+    def begin_chain(turn):
+        index = order(turn)
+
+        def store(columns, value):
+            part_out[index, :, columns] = value.astype(float_half)
+
+        @pl.when(outermost)
+        def _():
+            multiply(index, store)
+            part_copy(turn).start()
+
+    def continue_chain(turn):
+        index = order(turn)
+
+        def store(columns, value):
+            product[:, columns] = value
+
+        @pl.when(jnp.logical_not(outermost))
+        def _():
+            multiply(index, store)
+            part_arrival(index).wait_recv()
+            part_out[index] = (product[...] + part_in[index].astype(jnp.float32)).astype(
+                float_half
+            )
+            part_copy(turn).start()
+
+    def own_product():
+        def store(columns, value):
+            total[:, columns] = value
+
+        multiply(dp, store)
 
     for turn in range(n_dp + 2):
         if turn < n_dp:
+            index = order(turn)
             if turn:
-                grad_arrival(turn).wait_recv()
-            index = flip(dp, turn)
+                grad_arrival(index).wait_recv()
             for step in range(1, n_fsdp):
                 cross_copy(index, step).start()
             for side in range(1, n_core):
@@ -376,23 +424,32 @@
             project()
             loads[2].wait()
         if 1 <= turn <= n_dp:
-            index = flip(dp, turn - 1)
+            index = order(turn - 1)
             for step in range(1, n_fsdp):
                 cross_arrival(index, step).wait_recv()
                 for side in range(1, n_core):
                     core_copy(index, step, side).start()
         if turn >= 2:
-            index = flip(dp, turn - 2)
+            index = order(turn - 2)
             for step in range(n_fsdp):
                 for side in range(1, n_core):
                     core_arrival(index, step, side).wait_recv()
-            multiply(turn - 2)
-        if turn == 2:
-            adapter_gradients()
-
-    for step in range(1, n_dp):
-        part_arrival(step).wait_recv()
-        total[...] += part_in[flip(dp, step)].astype(jnp.float32)
+            if turn == 2:
+                own_product()
+                adapter_gradients()
+            else:
+                begin_chain(turn - 2)
+
+    for turn in range(1, n_dp):
+        continue_chain(turn)
+
+    for slot, there in ((dp, dp > 0), (n_dp, dp < n_dp - 1)):
+
+        @pl.when(there)
+        def _():
+            part_arrival(slot).wait_recv()
+            total[...] += part_in[slot].astype(jnp.float32)
+
     out_ref[...] = total[...].astype(float_half)
     for step in range(1, n_dp):
         dp_arrival(step, *back_args).wait_recv()
@@ -490,7 +547,8 @@
             pltpu.VMEM((n_feat, tok // n_feat, width), float_half),
             pltpu.VMEM((n_dp, tok, width_dp), float_half),
             pltpu.VMEM((n_dp, tok, feats), float_half),
-            pltpu.VMEM((n_dp, tok, feats), float_half),
+            pltpu.VMEM((n_dp + 1, tok, feats), float_half),
+            pltpu.VMEM((tok, feats), jnp.float32),
             pltpu.VMEM((tok, feats), jnp.float32),
             dma((3,)),
             *pair,
@@ -503,7 +561,8 @@
             dma((n_dp, n_fsdp)),
             dma((n_dp, n_fsdp, n_core)),
             dma((n_dp, n_fsdp, n_core)),
-            *pair,
+            dma((n_dp,)),
+            dma((n_dp + 1,)),
         ],
         compiler_params=pltpu.CompilerParams(
             collective_id=0, has_side_effects=True, vmem_limit_bytes=56 * 2**20

time: 155 us -> 131 us (0.85)
  the two profiles are of different devices: /device:TPU:18 before, /device:TPU:0 now
where the time goes in v3:
time: 131 us; the launch traced here: 129 us
  Pallas kernels  118 us (90%)
  matrix products  5.47 us (4%)
  other arithmetic  3.23 us (2%)
  local copies, waits for them, and re-layouts  1.77 us (1%)
    pallas_call x1, Pallas kernels, local(): pl.pallas_call(functools.partial(kernel, n_dp, n_fsdp, n_core, rank), out...  118 us
    dot_general x1, matrix products, local(): lax.dot_general(chosen, back[:, feats:], both_major, preferred_element_ty...  3.04 us

profile of v3, /device:TPU:0, one launch (start us, length us, event | category | flops | bytes accessed | tf_op | source)
XLA Modules:
  0.0 129.1 jit_solution(4973299618179746653)
XLA Ops:
  0.6 0.9 fusion.9
  1.5 0.1 select_reduce_fusion
  1.6 0.1 iota_compare_fusion.1
  1.7 0.1 broadcast_in_dim.54
  1.7 0.1 broadcast_in_dim.55
  1.8 0.7 fusion.2
  2.6 0.7 convert_reduce_fusion.mask_ref
  3.3 0.8 select_select_fusion.key_ref
  4.0 0.7 broadcast_in_dim.56.asked_ref
  4.8 118.0 %shard_map.103 = (bf16[384,1024]{1,0:T(8,128)(2,1)}, bf16[64,3072]{1,0:T(8,128)(2,1)}, bf16[64,512]{1,0:T(8,128)(2,1)}) custom-call(bf16[384,2048]{1,0:T(8,128)(2,1)} %grad_ref.1, bf16[384,1024]{1,0:T(8,128)(2,1)} %act_ref.1, bf16[1024,2048]{1,0:T(8,128)(2,1)} %weight_hbm.1, bf16[512,1024]{1,0:T(8,128)(2,1)} %bitcast.13, bf16[512,2048]{1,0:T(8,128)(2,1)} %bitcast.12, ...), custom_call_target="tpu_custom_call" | custom-call | flops 6442450944 | bytes 8912896 | tf_op jit(solution)/shard_map/pallas_call | solution.py:527
  122.8 0.0 copy-start
  122.8 2.4 %convolution_convert_fusion.1 = bf16[512,1024]{1,0:T(8,128)(2,1)} fusion(bf16[64,512]{1,0:T(8,128)(2,1)} %get-tuple-element.7, bf16[64,3072]{1,0:T(8,128)(2,1)} %get-tuple-element.8), kind=kOutput, calls=%fused_computation.1 | convolution fusion | flops 67633152 | bytes 1245184 | tf_op jit(solution)/shard_map/dot_general | solution.py:576
  125.2 3.0 %convolution_convert_fusion = bf16[512,2048]{1,0:T(8,128)(2,1)} fusion(bf16[64,512]{1,0:T(8,128)(2,1)} %get-tuple-element.7, bf16[64,3072]{1,0:T(8,128)(2,1)} %get-tuple-element.8), kind=kOutput, calls=%fused_computation | convolution fusion | flops 135266304 | bytes 2424832 | tf_op jit(solution)/shard_map/dot_general | solution.py:579
  128.2 0.0 copy-done
  128.2 0.9 copy.12
  (8 shorter events, 0.0 us)
Async XLA Ops:
  122.8 5.5 %copy-start = (bf16[384,1024]{1,0:T(8,128)(2,1)S(1)}, bf16[384,1024]{1,0:T(8,128)(2,1)}, u32[]{:S(2)}) copy-start(bf16[384,1024]{1,0:T(8,128)(2,1)} %get-tuple-element.22) | copy-start | bytes 2359300

commit v4 on v2

v4 whole, which is shorter than its diff:
```python
import functools

import jax
import jax.numpy as jnp
import numpy as np
from jax import lax
from jax.experimental import pallas as pl
from jax.experimental.pallas import tpu as pltpu
from jax.sharding import PartitionSpec as P

adapter_scale = 2.0
float_half = jnp.bfloat16
both_minor = (((1,), (1,)), ((), ()))
both_major = (((0,), (0,)), ((), ()))


def flip(index, step):
    out, bit = index, 1
    while bit <= step:
        if step & bit:
            out = out + bit - 2 * bit * ((index // bit) % 2)
        bit *= 2
    return out


def copy_to(src, dst, send_sem, recv_sem, device):
    return pltpu.make_async_remote_copy(
        src_ref=src,
        dst_ref=dst,
        send_sem=send_sem,
        recv_sem=recv_sem,
        device_id=device,
        device_id_type=pl.DeviceIdType.MESH,
    )


def kernel(
    n_dp,
    n_fsdp,
    n_core,
    rank,
    waves,
    grad_ref,
    act_ref,
    weight_hbm,
    down_hbm,
    up_hbm,
    key_ref,
    segment_ref,
    first_ref,
    row_ref,
    out_ref,
    back_ref,
    sel_ref,
    weight,
    down,
    up,
    asked_ref,
    asked_in,
    factor_out,
    factor_in,
    proj_out,
    proj_in,
    back_out,
    back_in,
    rows_in,
    grad_all,
    part_out,
    part_in,
    product,
    total,
    load_sem,
    asked_s,
    asked_r,
    factor_s,
    factor_r,
    proj_s,
    proj_r,
    back_s,
    back_r,
    rows_s,
    rows_r,
    grad_s,
    grad_r,
    cross_s,
    cross_r,
    core_s,
    core_r,
    part_s,
    part_r,
):
    dp, fsdp, core = lax.axis_index("dp"), lax.axis_index("fsdp"), lax.axis_index("adapter")
    feat = fsdp * n_core + core
    n_feat = n_fsdp * n_core
    tok, width = grad_ref.shape
    feats = act_ref.shape[1]
    wave_rows = tok // waves
    rows = wave_rows // n_feat
    width_dp = weight.shape[1]
    per_feat = n_dp // n_feat

    def feat_device(index):
        return {"fsdp": index // n_core, "adapter": index % n_core}

    def rank_rows(index):
        return pl.ds(pl.multiple_of(index * rank, rank), rank)

    def token_rows(wave, index):
        return pl.ds(pl.multiple_of(wave * wave_rows + index * rows, rows), rows)

    def wave_slice(wave):
        return pl.ds(wave * wave_rows, wave_rows)

    def share(wave, index, part):
        return grad_all.at[wave, pl.ds(pl.multiple_of(index * wave_rows + part * rows, rows), rows)]

    loads = [
        pltpu.make_async_copy(src, dst, load_sem.at[i])
        for i, (src, dst) in enumerate(((down_hbm, down), (up_hbm, up), (weight_hbm, weight)))
    ]
    for load in loads:
        load.start()

    barrier = pltpu.get_barrier_semaphore()
    for step in range(1, n_dp):
        pl.semaphore_signal(
            barrier,
            inc=1,
            device_id={"dp": flip(dp, step)},
            device_id_type=pl.DeviceIdType.MESH,
        )
    for step in range(1, n_feat):
        pl.semaphore_signal(
            barrier,
            inc=1,
            device_id=feat_device(flip(feat, step)),
            device_id_type=pl.DeviceIdType.MESH,
        )
    pl.semaphore_wait(barrier, n_dp + n_feat - 2)

    def dp_exchange(step, src, dst, send, recv):
        peer = flip(dp, step)
        return copy_to(
            src.at[rank_rows(peer)],
            dst.at[rank_rows(dp)],
            send.at[peer],
            recv.at[dp],
            {"dp": peer},
        )

    def dp_arrival(step, src, dst, send, recv):
        peer = flip(dp, step)
        return copy_to(
            src.at[rank_rows(peer)],
            dst.at[rank_rows(peer)],
            send.at[peer],
            recv.at[peer],
            {"dp": peer},
        )

    asked_args = (asked_ref, asked_in, asked_s, asked_r)
    factor_args = (factor_out, factor_in, factor_s, factor_r)
    back_args = (back_out, back_in, back_s, back_r)

    segs = first_ref.shape[0]
    table = up.shape[0] // rank
    table_rows = [row_ref[segment_ref[seg]] for seg in range(segs)]
    starts = [first_ref[seg] for seg in range(segs)]
    limits = starts[1:] + [tok]
    owned = []
    for owner in range(n_dp):
        wanted, start, limit = 0, 0, 0
        for seg in range(segs):
            local_row = table_rows[seg] - owner * table
            mine = (local_row >= 0) & (local_row < table)
            wanted += jnp.where(mine, local_row + 1, 0)
            start += jnp.where(mine, starts[seg], 0)
            limit += jnp.where(mine, limits[seg], 0)
        owned.append((start, limit))
        asked_ref[owner * rank : (owner + 1) * rank, :] = jnp.full(
            (rank, table * rank), wanted, jnp.int32
        )
    for step in range(1, n_dp):
        dp_exchange(step, *asked_args).start()
    asked_in[rank_rows(dp), :] = asked_ref[rank_rows(dp), :]

    def rows_copy(wave, step):
        peer = flip(feat, step)
        return copy_to(
            grad_ref.at[token_rows(wave, peer)],
            rows_in.at[wave, feat],
            rows_s.at[wave, peer],
            rows_r.at[wave, feat],
            feat_device(peer),
        )

    def rows_arrival(wave, step):
        peer = flip(feat, step)
        return copy_to(
            grad_ref.at[token_rows(wave, peer)],
            rows_in.at[wave, peer],
            rows_s.at[wave, peer],
            rows_r.at[wave, peer],
            feat_device(peer),
        )

    def spread_rows(wave):
        for step in range(1, n_feat):
            rows_copy(wave, step).start()

    def grad_copy(wave, step, part):
        source = flip(feat, step)
        target = source * per_feat + part
        columns = pl.ds(part * width_dp, width_dp)
        if step == 0:
            block = grad_ref.at[token_rows(wave, feat), columns]
        else:
            block = rows_in.at[wave, source, :, columns]
        copy = copy_to(
            block,
            share(wave, dp, feat),
            grad_s.at[wave, target],
            grad_r.at[wave, dp],
            {"dp": target},
        )
        return target, block, copy

    def forward(wave, step):
        for part in range(per_feat):
            target, block, copy = grad_copy(wave, step, part)

            @pl.when(target != dp)
            def _():
                copy.start()

            @pl.when(target == dp)
            def _():
                share(wave, dp, feat)[...] = block[...]

    spread_rows(0)
    forward(0, 0)

    def factors():
        loads[0].wait()
        loads[1].wait()
        for step in range(1, n_dp):
            dp_arrival(step, *asked_args).wait_recv()
        chosen = jnp.where(asked_in[...] - 1 == key_ref[...], 1.0, 0.0).astype(float_half)
        sel_ref[...] = chosen
        factor_out[:, :feats] = jnp.dot(
            chosen, down[...], preferred_element_type=jnp.float32
        ).astype(float_half)
        factor_out[:, feats:] = jnp.dot(
            chosen, up[...], preferred_element_type=jnp.float32
        ).astype(float_half)
        for step in range(1, n_dp):
            dp_exchange(step, *factor_args).start()
        factor_in[rank_rows(dp), :] = factor_out[rank_rows(dp), :]

    def proj_copy(step):
        peer = flip(feat, step)
        return copy_to(
            proj_out, proj_in.at[feat], proj_s.at[peer], proj_r.at[feat], feat_device(peer)
        )

    def proj_arrival(step):
        peer = flip(feat, step)
        return copy_to(
            proj_out, proj_in.at[peer], proj_s.at[peer], proj_r.at[peer], feat_device(peer)
        )

    def in_owner(owner):
        places = lax.broadcasted_iota(jnp.int32, (rank, tok), 1)
        start, limit = owned[owner]
        return (places >= start) & (places < limit)

    def project():
        for step in range(1, n_dp):
            dp_arrival(step, *factor_args).wait_recv()
        for half, (factor, value) in enumerate(
            ((factor_in[:, feats:], grad_ref[...]), (factor_in[:, :feats], act_ref[...]))
        ):
            product = lax.dot_general(
                factor, value, both_minor, preferred_element_type=jnp.float32
            )
            folded = jnp.zeros((rank, tok), jnp.float32)
            for owner in range(n_dp):
                folded += jnp.where(
                    in_owner(owner), product[owner * rank : (owner + 1) * rank], 0.0
                )
            proj_out[half * rank : (half + 1) * rank, :] = folded
        for step in range(1, n_feat):
            proj_copy(step).start()
        proj_in[feat] = proj_out[...]

    def adapter_gradients():
        for step in range(1, n_feat):
            proj_arrival(step).wait_recv()
        summed = proj_in[0]
        for index in range(1, n_feat):
            summed += proj_in[index]

        def spread(values):
            return jnp.concatenate(
                [jnp.where(in_owner(owner), values, 0.0) for owner in range(n_dp)], axis=0
            ).astype(float_half)

        up_block, down_block = spread(summed[:rank]), spread(summed[rank:])
        back_out[:, :feats] = (
            adapter_scale
            * jnp.dot(up_block, act_ref[...], preferred_element_type=jnp.float32)
        ).astype(float_half)
        back_out[:, feats:] = (
            adapter_scale
            * jnp.dot(down_block, grad_ref[...], preferred_element_type=jnp.float32)
        ).astype(float_half)
        for step in range(1, n_dp):
            dp_exchange(step, *back_args).start()
        back_in[rank_rows(dp), :] = back_out[rank_rows(dp), :]
        total[...] += adapter_scale * lax.dot_general(
            up_block, factor_in[:, :feats], both_major, preferred_element_type=jnp.float32
        )

    def grad_arrival(wave, peer):
        block = share(wave, peer, feat)
        return copy_to(block, block, grad_s.at[wave, peer], grad_r.at[wave, peer], {"dp": peer})

    def cross_copy(wave, index, step):
        peer = flip(fsdp, step)
        block = share(wave, index, feat)
        return copy_to(
            block,
            block,
            cross_s.at[wave, index, peer],
            cross_r.at[wave, index, fsdp],
            {"fsdp": peer},
        )

    def cross_arrival(wave, index, step):
        peer = flip(fsdp, step)
        block = share(wave, index, peer * n_core + core)
        return copy_to(
            block,
            block,
            cross_s.at[wave, index, peer],
            cross_r.at[wave, index, peer],
            {"fsdp": peer},
        )

    def core_copy(wave, index, step, side):
        chip, peer = flip(fsdp, step), flip(core, side)
        block = share(wave, index, chip * n_core + core)
        return copy_to(
            block,
            block,
            core_s.at[wave, index, chip, peer],
            core_r.at[wave, index, chip, core],
            {"adapter": peer},
        )

    def core_arrival(wave, index, step, side):
        chip, peer = flip(fsdp, step), flip(core, side)
        block = share(wave, index, chip * n_core + peer)
        return copy_to(
            block,
            block,
            core_s.at[wave, index, chip, peer],
            core_r.at[wave, index, chip, peer],
            {"adapter": peer},
        )

    def order(turn):
        if turn == 0:
            return dp
        upper = dp // (n_dp // 2)
        falling, rising = n_dp - turn, turn - 1
        falling = falling - (dp - falling + n_dp) // n_dp
        rising = rising + (rising - dp + n_dp) // n_dp
        return (1 - upper) * falling + upper * rising

    def part_copy(wave, turn):
        index = order(turn)
        above = (index - dp - 1 + n_dp) // n_dp
        following = dp + 2 * above - 1
        ends = (1 - above) * (1 - (following - index + n_dp - 1) // n_dp)
        slot = index + ends * (n_dp - index)
        return copy_to(
            part_out.at[wave, index],
            part_in.at[wave, slot],
            part_s.at[wave, index],
            part_r.at[wave, slot],
            {"dp": following},
        )

    def part_arrival(wave, slot):
        return copy_to(
            part_out.at[wave, 0],
            part_in.at[wave, slot],
            part_s.at[wave, 0],
            part_r.at[wave, slot],
            {"dp": flip(dp, 1)},
        )

    tile = 256 if feats % 256 == 0 else feats
    outermost = dp * (n_dp - 1 - dp) == 0

    def rows_of(index):
        return pl.ds(pl.multiple_of(index * wave_rows, wave_rows), wave_rows)

    def forward_all(wave):
        if wave + 1 < waves:
            spread_rows(wave + 1)
        if wave:
            forward(wave, 0)
        for step in range(1, n_feat):
            rows_arrival(wave, step).wait_recv()
            forward(wave, step)

    def collect(wave):
        for turn in range(n_dp):
            index = order(turn)
            if turn:
                grad_arrival(wave, index).wait_recv()
            for step in range(1, n_fsdp):
                cross_copy(wave, index, step).start()
            for side in range(1, n_core):
                core_copy(wave, index, 0, side).start()

    def hand_over(wave):
        for turn in range(n_dp):
            index = order(turn)
            for step in range(1, n_fsdp):
                cross_arrival(wave, index, step).wait_recv()
                for side in range(1, n_core):
                    core_copy(wave, index, step, side).start()

    def multiply(wave):
        for turn in range(n_dp):
            for step in range(n_fsdp):
                for side in range(1, n_core):
                    core_arrival(wave, order(turn), step, side).wait_recv()

        def one(i, carry):
            columns = pl.ds(pl.multiple_of(i * tile, tile), tile)
            product[:, columns] = lax.dot_general(
                grad_all[wave], weight[columns, :], both_minor, preferred_element_type=jnp.float32
            )
            return carry

        lax.fori_loop(0, feats // tile, one, 0)

        @pl.when(outermost)
        def _():
            for turn in range(1, n_dp):
                index = order(turn)
                part_out[wave, index] = product[rows_of(index), :].astype(float_half)
                part_copy(wave, turn).start()

        total[wave_slice(wave), :] += product[rows_of(dp), :]

    def chain(wave):
        @pl.when(jnp.logical_not(outermost))
        def _():
            for turn in range(1, n_dp):
                index = order(turn)
                part_arrival(wave, index).wait_recv()
                part_out[wave, index] = (
                    product[rows_of(index), :] + part_in[wave, index].astype(jnp.float32)
                ).astype(float_half)
                part_copy(wave, turn).start()

    total[...] = jnp.zeros_like(total)
    forward_all(0)
    for wave in range(1, waves + 3):
        if wave < waves:
            forward_all(wave)
        if wave == 1:
            factors()
        if 0 <= wave - 1 < waves:
            collect(wave - 1)
        if wave == 2:
            project()
            loads[2].wait()
        if 0 <= wave - 2 < waves:
            hand_over(wave - 2)
        if 0 <= wave - 3 < waves:
            chain(wave - 3)
        if 0 <= wave - 2 < waves:
            multiply(wave - 2)
        if wave == 3:
            adapter_gradients()

    for wave in range(waves):
        for slot, there in ((dp, dp > 0), (n_dp, dp < n_dp - 1)):

            @pl.when(there)
            def _():
                part_arrival(wave, slot).wait_recv()
                total[wave_slice(wave), :] += part_in[wave, slot].astype(jnp.float32)

    out_ref[...] = total[...].astype(float_half)
    for step in range(1, n_dp):
        dp_arrival(step, *back_args).wait_recv()
    back_ref[...] = back_in[...]

    for step in range(1, n_dp):
        for args in (asked_args, factor_args, back_args):
            dp_exchange(step, *args).wait_send()
    for step in range(1, n_feat):
        proj_copy(step).wait_send()
    for wave in range(waves):
        for step in range(1, n_dp):
            part_copy(wave, step).wait_send()
        for step in range(1, n_feat):
            rows_copy(wave, step).wait_send()
        for step in range(n_feat):
            for part in range(per_feat):
                target, _, copy = grad_copy(wave, step, part)

                @pl.when(target != dp)
                def _():
                    copy.wait_send()

        for turn in range(n_dp):
            index = flip(dp, turn)
            for step in range(1, n_fsdp):
                cross_copy(wave, index, step).wait_send()
            for step in range(n_fsdp):
                for side in range(1, n_core):
                    core_copy(wave, index, step, side).wait_send()


def place(chosen_ref, back_ref, in_ref, a_ref, b_ref, out_ref):
    feats = a_ref.shape[1]
    a_ref[...] = lax.dot_general(
        chosen_ref[...], back_ref[:, :feats], both_major, preferred_element_type=jnp.float32
    ).astype(float_half)
    b_ref[...] = lax.dot_general(
        chosen_ref[...], back_ref[:, feats:], both_major, preferred_element_type=jnp.float32
    ).astype(float_half)
    out_ref[...] = in_ref[...]


def local(
    output_gradient,
    attention_output,
    frozen_weight,
    adapter_down_table,
    adapter_up_table,
    segment_adapter,
    segment_first_token,
    adapter_table_row,
):
    n_dp, n_fsdp, n_core = (lax.axis_size(name) for name in ("dp", "fsdp", "adapter"))
    n_feat = n_fsdp * n_core
    tok, width = output_gradient.shape
    table, feats, rank = adapter_down_table.shape
    width_dp = frozen_weight.shape[1]
    row_of = np.arange(n_dp * rank, dtype=np.int32)[:, None]
    col_of = np.arange(table * rank, dtype=np.int32)[None, :]
    key = jnp.asarray(
        np.where(row_of % rank == col_of % rank, col_of // rank, -5).astype(np.int32)
    )
    down = jnp.transpose(adapter_down_table, (0, 2, 1)).reshape(table * rank, feats)
    up = adapter_up_table.reshape(table * rank, width)
    both = feats + width
    waves = 3 if tok % (3 * 16 * n_feat) == 0 else 1
    vmem = pl.BlockSpec(memory_space=pltpu.VMEM)
    hbm = pl.BlockSpec(memory_space=pl.ANY)
    smem = pl.BlockSpec(memory_space=pltpu.SMEM)
    dma = pltpu.SemaphoreType.DMA
    pair = [dma((n_dp,)), dma((n_dp,))]
    feat_pair = [dma((n_feat,)), dma((n_feat,))]
    input_gradient, back, chosen = pl.pallas_call(
        functools.partial(kernel, n_dp, n_fsdp, n_core, rank, waves),
        out_shape=(
            jax.ShapeDtypeStruct((tok, feats), float_half),
            jax.ShapeDtypeStruct((n_dp * rank, both), float_half),
            jax.ShapeDtypeStruct((n_dp * rank, table * rank), float_half),
        ),
        in_specs=[vmem, vmem, hbm, hbm, hbm, vmem, smem, smem, smem],
        out_specs=[vmem] * 3,
        scratch_shapes=[
            pltpu.VMEM((feats, width_dp), float_half),
            pltpu.VMEM((table * rank, feats), float_half),
            pltpu.VMEM((table * rank, width), float_half),
            pltpu.VMEM((n_dp * rank, table * rank), jnp.int32),
            pltpu.VMEM((n_dp * rank, table * rank), jnp.int32),
            pltpu.VMEM((n_dp * rank, both), float_half),
            pltpu.VMEM((n_dp * rank, both), float_half),
            pltpu.VMEM((2 * rank, tok), jnp.float32),
            pltpu.VMEM((n_feat, 2 * rank, tok), jnp.float32),
            pltpu.VMEM((n_dp * rank, both), float_half),
            pltpu.VMEM((n_dp * rank, both), float_half),
            pltpu.VMEM((waves, n_feat, tok // waves // n_feat, width), float_half),
            pltpu.VMEM((waves, n_dp * tok // waves, width_dp), float_half),
            pltpu.VMEM((waves, n_dp, tok // waves, feats), float_half),
            pltpu.VMEM((waves, n_dp + 1, tok // waves, feats), float_half),
            pltpu.VMEM((n_dp * tok // waves, feats), jnp.float32),
            pltpu.VMEM((tok, feats), jnp.float32),
            dma((3,)),
            *pair,
            *pair,
            *feat_pair,
            *pair,
            dma((waves, n_feat)),
            dma((waves, n_feat)),
            dma((waves, n_dp)),
            dma((waves, n_dp)),
            dma((waves, n_dp, n_fsdp)),
            dma((waves, n_dp, n_fsdp)),
            dma((waves, n_dp, n_fsdp, n_core)),
            dma((waves, n_dp, n_fsdp, n_core)),
            dma((waves, n_dp)),
            dma((waves, n_dp + 1)),
        ],
        compiler_params=pltpu.CompilerParams(
            collective_id=0, has_side_effects=True, vmem_limit_bytes=56 * 2**20
        ),
        cost_estimate=pl.CostEstimate(
            flops=2 * n_dp * tok * width_dp * feats,
            bytes_accessed=2 * (feats * width_dp + 2 * tok * (width + feats)),
            transcendentals=0,
        ),
    )(
        output_gradient,
        attention_output,
        frozen_weight,
        down,
        up,
        key,
        segment_adapter,
        segment_first_token,
        adapter_table_row,
    )
    steps = 4
    slots, tokens = table * rank // steps, tok // steps
    grad_a, grad_b, input_gradient = pl.pallas_call(
        place,
        grid=(steps,),
        out_shape=(
            jax.ShapeDtypeStruct((table * rank, feats), float_half),
            jax.ShapeDtypeStruct((table * rank, width), float_half),
            jax.ShapeDtypeStruct((tok, feats), float_half),
        ),
        in_specs=[
            pl.BlockSpec((n_dp * rank, slots), lambda i: (0, i)),
            pl.BlockSpec((n_dp * rank, both), lambda i: (0, 0)),
            pl.BlockSpec((tokens, feats), lambda i: (i, 0)),
        ],
        out_specs=[
            pl.BlockSpec((slots, feats), lambda i: (i, 0)),
            pl.BlockSpec((slots, width), lambda i: (i, 0)),
            pl.BlockSpec((tokens, feats), lambda i: (i, 0)),
        ],
        compiler_params=pltpu.CompilerParams(vmem_limit_bytes=32 * 2**20),
    )(chosen, back, input_gradient)
    grad_a = jnp.transpose(grad_a.reshape(table, rank, feats), (0, 2, 1))
    return input_gradient, grad_a, grad_b.reshape(table, rank, width)


def solution(mesh):
    in_specs = (
        P(("groups", "dp"), ("fsdp", "adapter")),
        P(("groups", "dp"), ("fsdp", "adapter")),
        P(("fsdp", "adapter"), "dp"),
        P(("groups", "dp"), ("fsdp", "adapter"), None),
        P(("groups", "dp"), None, ("fsdp", "adapter")),
        P(("groups", "dp")),
        P(("groups", "dp")),
        P("groups"),
    )
    out_specs = (
        P(("groups", "dp"), ("fsdp", "adapter")),
        P(("groups", "dp"), ("fsdp", "adapter"), None),
        P(("groups", "dp"), None, ("fsdp", "adapter")),
    )
    return jax.shard_map(local, mesh=mesh, in_specs=in_specs, out_specs=out_specs, check_vma=False)
```

time: 155 us -> 125 us (0.81)
  the two profiles are of different devices: /device:TPU:18 before, /device:TPU:0 now
where the time goes in v4:
time: 125 us
  Pallas kernels  121 us (97%)
  local copies, waits for them, and re-layouts  2.96 us (2%)
    pallas_call x1, Pallas kernels, local(): pl.pallas_call(functools.partial(kernel, n_dp, n_fsdp, n_core, rank, wave...  118 us
    unnamed x6, local copies, waits for them, and re-layouts  2.96 us
    pallas_call x1, Pallas kernels, local(): pl.pallas_call(place, grid=(steps,), out_shape=(jax.ShapeDtypeStruct((tab...  2.9 us

profile of v4, /device:TPU:0, one launch (start us, length us, event | category | flops | bytes accessed | tf_op | source)
XLA Modules:
  0.0 124.6 jit_solution(16125757472981102357)
XLA Ops:
  0.6 118.1 %shard_map.112 = (bf16[384,1024]{1,0:T(8,128)(2,1)}, bf16[64,3072]{1,0:T(8,128)(2,1)}, bf16[64,512]{1,0:T(8,128)(2,1)}) custom-call(bf16[384,2048]{1,0:T(8,128)(2,1)} %grad_ref.1, bf16[384,1024]{1,0:T(8,128)(2,1)} %act_ref.1, bf16[1024,2048]{1,0:T(8,128)(2,1)} %weight_hbm.1, bf16[512,1024]{1,0:T(8,128)(2,1)} %bitcast.10, bf16[512,2048]{1,0:T(8,128)(2,1)} %bitcast.8, ...), custom_call_target="tpu_custom_call" | custom-call | flops 6442450944 | bytes 8912896 | tf_op jit(solution)/shard_map/pallas_call | solution.py:574
  118.8 0.0 copy-start
  118.8 1.1 copy-done
  119.9 0.0 copy-start.1
  119.9 1.0 copy-done.1
  120.9 0.0 copy-start.2
  120.9 0.8 copy-done.2
  121.7 2.9 %shard_map.113 = (bf16[512,1024]{1,0:T(8,128)(2,1)}, bf16[512,2048]{1,0:T(8,128)(2,1)}, bf16[384,1024]{1,0:T(8,128)(2,1)}) custom-call(bf16[64,512]{1,0:T(8,128)(2,1)S(1)} %copy-done.2, bf16[64,3072]{1,0:T(8,128)(2,1)S(1)} %copy-done.1, bf16[384,1024]{1,0:T(8,128)(2,1)S(1)} %copy-done), custom_call_target="tpu_custom_call" | custom-call | tf_op jit(solution)/shard_map/pallas_call | solution.py:638
Async XLA Ops:
  118.8 1.1 copy-start
  119.9 1.0 copy-start.1
  120.9 0.8 copy-start.2
